TPU v7x, 256 devices: a whole 4x4x8 slice. The times are simulated.
256 devices in a mesh: tm: 8 (over z_lo, core), height: 32 (over x, y, z_hi).
Axes of the slice: x: 4, y: 4, z: 8 (z_hi: 2, z_lo: 4; z = z_hi * 4 + z_lo), core: 2. Of those that a mesh axis runs over, the one named last changes fastest.
Arguments:
- clean_latents: bfloat16 [32, 128, 16, 3072], P('tm', 'height'), may hold values from -6 to 6
- gaussian_noise: bfloat16 [32, 128, 16, 3072], P('tm', 'height'), may hold values from -6 to 6
- text_states: bfloat16 [256, 3072], replicated, may hold values from -6 to 6
- queries: bfloat16 [32, 128, 16, 1536], P('tm', 'height'), may hold values from -40 to 40
- key_states: bfloat16 [32, 128, 16, 1536], P('tm', 'height'), may hold values from -8 to 8
- cotangent: bfloat16 [32, 128, 16, 1536], P('tm', 'height'), may hold values from -240 to 240
- text_keys: bfloat16 [256, 1536], replicated, may hold values from -6 to 6
- window_radii: int32 [12, 3], replicated, may hold values from 0 to 1
- timestep: int32 [1], replicated, may hold values from 200 to 799
- sketch_seed: int32 [1], replicated, may hold values from 0 to 65535
- down_image: bfloat16 [3072, 16], replicated, may hold values from -0.109375 to 0.109375
- up_image: bfloat16 [16, 1536], replicated, may hold values from -1.5 to 1.5
- down_text: bfloat16 [3072, 16], replicated, may hold values from -0.109375 to 0.109375
- up_text: bfloat16 [16, 1536], replicated, may hold values from -1.5 to 1.5
Outputs:
- value_grad: bfloat16 [32, 128, 16, 1536], P('tm', 'height')
- grad_sketch: float32 [16384], replicated
All inputs are finite; a program needn't handle non-finite values.
Results may differ from a plain program's by a relative error of at most 0.0075.
Values may be sent and summed in bfloat16 or wider, within the bound.
A program may use at most 128 MiB of HBM per device.

v0:
```python
import jax
import jax.numpy as jnp
from jax import lax
from jax.sharding import PartitionSpec as P

SKETCH = 16384
TW = 8


def padded_2(block, sides, width):
    for axis, dim in sides:
        count = lax.axis_size(axis)
        forward = [(i, i + 1) for i in range(count - 1)]
        backward = [(target, source) for source, target in forward]
        low = lax.ppermute(
            lax.slice_in_dim(block, block.shape[dim] - width, None, axis=dim), axis, forward
        )
        high = lax.ppermute(lax.slice_in_dim(block, 0, width, axis=dim), axis, backward)
        block = jnp.concatenate([low, block, high], axis=dim)
    return block


def shifted(array, axis, by):
    size = lax.axis_size(axis)
    pairs = [(i, i + by) for i in range(size) if 0 <= i + by < size]
    return lax.ppermute(array, axis, pairs)


def tile_rows(block, width):
    frame_count, row_count, col_count = (block.shape[0], block.shape[1], block.shape[2])
    rest = block.shape[3:]
    col_tiles = col_count // width
    shaped = block.reshape((frame_count, row_count, col_tiles, width) + rest)
    order = (2, 0, 1, 3) + tuple(range(4, 4 + len(rest)))
    return jnp.transpose(shaped, order).reshape((col_tiles, frame_count * row_count * width) + rest)


def region_rows(padded, width):
    col_count = padded.shape[2] - 2 * width
    views = [
        tile_rows(padded[:, :, shift_col * width : shift_col * width + col_count], width)
        for shift_col in range(3)
    ]
    return jnp.concatenate(views, axis=1)


def window_mask(
    radius, frame_tile, row_tile, frame_tiles, row_tiles, col_tiles, frame_count, row_count, width
):
    region = 27 * frame_count * row_count * width
    position = jnp.arange(region, dtype=jnp.int32)
    col_step = position // (9 * frame_count * row_count * width) - 1
    frame_step = position // (3 * row_count * width) % (3 * frame_count) // frame_count - 1
    row_step = position // width % (3 * row_count) // row_count - 1
    inside = (
        (jnp.abs(frame_step) <= radius[0])
        & (jnp.abs(row_step) <= radius[1])
        & (jnp.abs(col_step) <= radius[2])
    )
    inside = inside & (frame_tile + frame_step >= 0) & (frame_tile + frame_step < frame_tiles)
    inside = inside & (row_tile + row_step >= 0) & (row_tile + row_step < row_tiles)
    col_index = jnp.arange(col_tiles, dtype=jnp.int32)[:, None]
    return (
        inside[None, :]
        & (col_index + col_step[None, :] >= 0)
        & (col_index + col_step[None, :] < col_tiles)
    )


def forward_head(query_head, key_region, text_head, cot_head, allowed, score_scale):
    image_scores = (
        jnp.einsum("cqd,cld->cql", query_head, key_region, preferred_element_type=jnp.float32)
        * score_scale
    )
    image_scores = jnp.where(allowed[:, None, :], image_scores, -jnp.inf)
    text_scores = (
        jnp.einsum("cqd,td->cqt", query_head, text_head, preferred_element_type=jnp.float32)
        * score_scale
    )
    row_max = jnp.maximum(jnp.max(image_scores, axis=-1), jnp.max(text_scores, axis=-1))
    total = jnp.sum(jnp.exp(image_scores - row_max[..., None]), axis=-1) + jnp.sum(
        jnp.exp(text_scores - row_max[..., None]), axis=-1
    )
    log_total = row_max + jnp.log(total)
    text_probs = jnp.exp(text_scores - log_total[..., None]).astype(jnp.bfloat16)
    text_part = jnp.einsum("cqt,cqd->td", text_probs, cot_head, preferred_element_type=jnp.float32)
    return (image_scores, log_total, text_part)


def place_back(spread, frame_count, row_count, width):
    col_tiles, head_width = (spread.shape[0], spread.shape[2])
    shaped = spread.reshape(col_tiles, 3, 3 * frame_count, 3 * row_count, width, head_width)
    placed = jnp.zeros((3 * frame_count, 3 * row_count, col_tiles, width, head_width), jnp.float32)
    for shift_col in range(3):
        moved = jnp.transpose(shaped[:, shift_col], (1, 2, 0, 3, 4))
        moved = jnp.pad(moved, ((0, 0), (0, 0), (1, 1), (0, 0), (0, 0)))
        placed = placed + moved[:, :, 2 - shift_col : 2 - shift_col + col_tiles]
    return placed.reshape(3 * frame_count, 3 * row_count, col_tiles * width, head_width)


def sketch_signs(seed_value, rows, width):
    row_part = jnp.arange(rows, dtype=jnp.int32)[:, None] * width
    position = row_part + jnp.arange(width, dtype=jnp.int32)[None, :]
    mixed_bits = position * 1103515245 + seed_value * 12345 + 1013904223
    mixed_bits = mixed_bits ^ mixed_bits >> 16
    mixed_bits = mixed_bits * 73244475
    mixed_bits = mixed_bits ^ mixed_bits >> 16
    return (1 - 2 * (mixed_bits >> 7 & 1)).astype(jnp.float32)


def count_sketch(pieces, seed_value, width, sketch_scale):
    flat = jnp.concatenate([piece.reshape(-1) for piece in pieces]).reshape(-1, width)
    signed = flat * sketch_signs(seed_value, flat.shape[0], width)
    return jnp.sum(signed, axis=0) * sketch_scale


def text_grads(text_hidden, text_value, text_states, up_text):
    highest = lax.Precision.HIGHEST
    text_up_grad = jnp.dot(text_hidden.T, text_value, precision=highest)
    text_back = jnp.dot(text_value, up_text.astype(jnp.float32).T, precision=highest)
    text_down_grad = jnp.dot(text_states.astype(jnp.float32).T, text_back, precision=highest)
    return (text_down_grad, text_up_grad)


def per_device(
    clean_latents,
    gaussian_noise,
    text_states,
    queries,
    key_states,
    cotangent,
    text_keys,
    window_radii,
    timestep,
    sketch_seed,
    down_image,
    up_image,
    down_text,
    up_text,
):
    frame_count, row_count, col_count, value_width = queries.shape
    head_count = window_radii.shape[0]
    head_width = value_width // head_count
    col_tiles = col_count // TW
    score_scale = head_width ** (-0.5)
    frame_tile = lax.axis_index("tm")
    row_tile = lax.axis_index("height")
    frame_tiles = lax.axis_size("tm")
    row_tiles = lax.axis_size("height")
    pad_spec = ((0, 0), (0, 0), (TW, TW), (0, 0))
    key_pad = jnp.pad(padded_2(key_states, (("tm", 0), ("height", 1)), frame_count), pad_spec)
    own_q = tile_rows(queries, TW)
    own_c = tile_rows(cotangent, TW)
    head_ids = jnp.arange(head_count, dtype=jnp.int32)

    def head_mask(head_index):
        return window_mask(
            window_radii[head_index],
            frame_tile,
            row_tile,
            frame_tiles,
            row_tiles,
            col_tiles,
            frame_count,
            row_count,
            TW,
        )

    def forward(head_index):
        offset = head_index * head_width
        allowed = head_mask(head_index)
        query_head = lax.dynamic_slice_in_dim(own_q, offset, head_width, 2)
        cot_head = lax.dynamic_slice_in_dim(own_c, offset, head_width, 2)
        key_region = region_rows(lax.dynamic_slice_in_dim(key_pad, offset, head_width, 3), TW)
        text_head = lax.dynamic_slice_in_dim(text_keys, offset, head_width, 1)
        image_scores, log_total, text_part = forward_head(
            query_head, key_region, text_head, cot_head, allowed, score_scale
        )
        image_probs = jnp.exp(image_scores - log_total[..., None]).astype(jnp.bfloat16)
        spread = jnp.einsum(
            "cql,cqd->cld", image_probs, cot_head, preferred_element_type=jnp.float32
        )
        return (text_part, place_back(spread, frame_count, row_count, TW))

    text_part, head_out = lax.map(forward, head_ids)
    text_value = jnp.transpose(text_part, (1, 0, 2)).reshape(-1, value_width)
    middle = head_out[:, :, row_count : 2 * row_count]
    for direction, border in (
        (-1, head_out[:, :, :row_count]),
        (1, head_out[:, :, 2 * row_count :]),
    ):
        middle = middle + shifted(border.astype(jnp.bfloat16), "height", direction).astype(
            border.dtype
        )
    own_part = middle[:, frame_count : 2 * frame_count]
    for direction, border in ((-1, middle[:, :frame_count]), (1, middle[:, 2 * frame_count :])):
        own_part = own_part + shifted(border.astype(jnp.bfloat16), "tm", direction).astype(
            border.dtype
        )
    value_f32 = jnp.transpose(own_part, (1, 2, 3, 0, 4)).reshape(
        frame_count, row_count, col_count, value_width
    )
    value_grad = value_f32.astype(jnp.bfloat16)
    noise_level = timestep[0].astype(jnp.float32) / 1000.0
    mixed = (
        (1.0 - noise_level) * clean_latents.astype(jnp.float32)
        + noise_level * gaussian_noise.astype(jnp.float32)
    ).astype(jnp.bfloat16)
    mixed = mixed.reshape(-1, mixed.shape[3])
    flat_value = value_grad.reshape(-1, value_width)
    hidden = jnp.dot(mixed, down_image, preferred_element_type=jnp.float32).astype(jnp.bfloat16)
    grad_up = lax.dot_general(
        hidden, flat_value, (((0,), (0,)), ((), ())), preferred_element_type=jnp.float32
    )
    backward_low = lax.dot_general(
        flat_value, up_image, (((1,), (1,)), ((), ())), preferred_element_type=jnp.float32
    ).astype(jnp.bfloat16)
    grad_down = lax.dot_general(
        mixed, backward_low, (((0,), (0,)), ((), ())), preferred_element_type=jnp.float32
    )
    text_hidden = jnp.dot(text_states, down_text, preferred_element_type=jnp.float32)
    token_total = frame_count * row_count * col_count * frame_tiles * row_tiles
    param_total = 2 * grad_down.size + 2 * grad_up.size
    sketch_scale = (token_total * (param_total // SKETCH)) ** (-0.5)
    text_down_grad, text_up_grad = text_grads(text_hidden, text_value, text_states, up_text)
    local_sketch = count_sketch(
        (grad_down, grad_up, text_down_grad, text_up_grad), sketch_seed[0], SKETCH, sketch_scale
    )
    grad_sketch = lax.psum(local_sketch, ("tm", "height"))
    return (value_grad, grad_sketch)


def solution(mesh):
    return jax.shard_map(
        per_device,
        mesh=mesh,
        in_specs=(
            P("tm", "height", None, None),
            P("tm", "height", None, None),
            P(),
            P("tm", "height", None, None),
            P("tm", "height", None, None),
            P("tm", "height", None, None),
            P(),
            P(),
            P(),
            P(),
            P(),
            P(),
            P(),
            P(),
        ),
        out_specs=(P("tm", "height", None, None), P()),
        check_vma=False,
    )
```

profile of v0, /device:TPU:1, one launch (start us, length us, event | category | flops | bytes accessed | tf_op | source)
XLA Modules:
  0.0 920.2 jit_solution(15900157499959258757)
XLA Ops:
  7.2 5.1 collective-permute-start
  12.3 1.9 collective-permute-start.1
  14.2 7.3 collective-permute-done
  22.5 2.1 constant_dynamic-update-slice_fusion.1
  28.1 12.5 %collective-permute-start.2 = (bf16[12,4,16,1536]{3,2,1,0:T(8,128)(2,1)}, bf16[12,4,16,1536]{3,2,1,0:T(8,128)(2,1)}, u32[]{:S(2)}, u32[]{:S(2)}) collective-permute-start(bf16[12,4,16,1536]{3,2,1,0:T(8,128)(2,1)} %constant_dynamic-update-slice_fusion), channel_id=1, source_target_pairs={{0,1},{1,2},{2,3},{3,4},{4,5},{5,6},{6,7},{7,8},{8,9},{9,10},{10,1... | collective-permute-start | bytes 7077896 | tf_op jit(solution)/shard_map/ppermute | solution.py:15
  40.7 2.1 copy.51
  42.8 97.1 %collective-permute-done.3 = bf16[12,4,16,1536]{3,2,1,0:T(8,128)(2,1)} collective-permute-done((bf16[12,4,16,1536]{3,2,1,0:T(8,128)(2,1)}, bf16[12,4,16,1536]{3,2,1,0:T(8,128)(2,1)}, u32[]{:S(2)}, u32[]{:S(2)}) %collective-permute-start.3) | collective-permute-done | bytes 2359328 | tf_op jit(solution)/shard_map/ppermute | solution.py:18
  139.9 9.7 %fusion.52 = bf16[12,12,32,1536]{3,2,1,0:T(8,128)(2,1)} fusion(bf16[12,4,16,1536]{3,2,1,0:T(8,128)(2,1)} %collective-permute-done.3, bf16[12,4,16,1536]{3,2,1,0:T(8,128)(2,1)} %constant_dynamic-update-slice_fusion, bf16[12,4,16,1536]{3,2,1,0:T(8,128)(2,1)} %collective-permute-done.2), kind=kLoop, calls=%fused_computation.99 | loop fusion | flops 84934656 | bytes 21233664 | tf_op jit(solution)/shard_map/concatenate | solution.py:19
  149.6 213.1 %while.15 = (s32[]{:T(128)}, f32[12,256,128]{1,2,0:T(8,128)}, f32[12,12,12,16,128]{4,3,2,1,0:T(8,128)}, s32[12]{0:T(128)S(1)}, bf16[2,128,1536]{2,1,0:T(8,128)(2...) while((s32[]{:T(128)}, f32[12,256,128]{1,2,0:T(8,128)}, ...), condition=%wide.region_5.6_spmd, body=%wide.region_0.5_spmd.sunk | while | flops 499376128 | bytes 40042176 | solution.py:185
  169.7 1.9 dynamic-slice_bitcast_fusion.4
  187.6 2.0 dynamic-slice_bitcast_fusion.4
  193.3 1.9 compare_and_fusion.4
  228.6 1.9 compare_and_fusion.4
  258.5 2.0 dynamic-slice_bitcast_fusion.4
  282.0 1.9 compare_and_fusion.4
  347.4 2.0 dynamic-slice_bitcast_fusion.4
  353.1 1.9 compare_and_fusion.4
  362.7 9.7 %convert.8 = bf16[12,12,12,16,128]{4,3,2,1,0:T(8,128)(2,1)} convert(f32[12,12,12,16,128]{4,3,2,1,0:T(8,128)} %get-tuple-element.191) | non-fusion elementwise | flops 3538944 | bytes 21233664 | tf_op jit(solution)/shard_map/convert.3
  372.4 6.3 fusion.75
  378.7 42.7 %collective-permute-start.5 = (bf16[12,12,4,16,128]{4,3,2,1,0:T(8,128)(2,1)}, bf16[12,12,4,16,128]{4,3,2,1,0:T(8,128)(2,1)}, u32[]{:S(2)}, u32[]{:S(2)}) collective-permute-start(bf16[12,12,4,16,128]{4,3,2,1,0:T(8,128)(2,1)} %get-tuple-element.230), channel_id=1, source_target_pairs={{0,1},{1,2},{2,3},{3,4},{4,5},{5,6},{6,7},{7,8},{8,9},{9,10},{10,1... | collective-permute-start | bytes 7077896 | tf_op jit(solution)/shard_map/ppermute | solution.py:26
  424.5 2.6 add_convert_fusion
  427.1 34.4 %collective-permute-done.5 = bf16[12,12,4,16,128]{4,3,2,1,0:T(8,128)(2,1)} collective-permute-done((bf16[12,12,4,16,128]{4,3,2,1,0:T(8,128)(2,1)}, bf16[12,12,4,16,128]{4,3,2,1,0:T(8,128)(2,1)}, u32[]{:S(2)}, u32[]{:S(2)}) %collective-permute-start.5) | collective-permute-done | bytes 2359328 | tf_op jit(solution)/shard_map/ppermute | solution.py:26
  461.5 108.8 %collective-permute-done.4 = bf16[12,12,4,16,128]{4,3,2,1,0:T(8,128)(2,1)} collective-permute-done((bf16[12,12,4,16,128]{4,3,2,1,0:T(8,128)(2,1)}, bf16[12,12,4,16,128]{4,3,2,1,0:T(8,128)(2,1)}, u32[]{:S(2)}, u32[]{:S(2)}) %collective-permute-start.4) | collective-permute-done | bytes 2359328 | tf_op jit(solution)/shard_map/ppermute | solution.py:26
  570.3 7.4 fusion.71
  579.3 61.7 %collective-permute-start.7 = (bf16[12,4,4,16,128]{4,3,2,1,0:T(8,128)(2,1)}, bf16[12,4,4,16,128]{4,3,2,1,0:T(8,128)(2,1)}, u32[]{:S(2)}, u32[]{:S(2)}) collective-permute-start(bf16[12,4,4,16,128]{4,3,2,1,0:T(8,128)(2,1)} %get-tuple-element.232), channel_id=1, source_target_pairs={{0,32},{32,64},{64,96},{96,128},{128,160},{160,192},{192,224},{1,3... | collective-permute-start | bytes 2359304 | tf_op jit(solution)/shard_map/ppermute | solution.py:26
  641.1 2.1 collective-permute-start.6
  644.6 2.0 fusion.77
  650.9 3.8 collective-permute-done.6
  654.7 2.2 fusion.54
  659.3 2.2 fusion.55
  662.2 3.7 fusion.56
  672.2 239.7 %all-reduce.5.cloned.1.call-done = f32[16384]{0:T(1024)} async-done(((f32[16384]{0:T(1024)}), f32[16384]{0:T(1024)}) %all-reduce.5.cloned.1.call-update) | async-done | bytes 65552 | tf_op jit(solution)/shard_map/psum | solution.py:229
  (328 shorter events, 190.9 us)
Async XLA Ops:
  7.2 416.8 %copy-start = (bf16[256,3072]{1,0:T(8,128)(2,1)S(1)}, bf16[256,3072]{1,0:T(8,128)(2,1)}, u32[]{:S(2)}) copy-start(bf16[256,3072]{1,0:T(8,128)(2,1)} %param.18) | copy-start | bytes 4718596
  7.2 33.5 %copy-start.6 = (bf16[4,4,16,1536]{3,2,1,0:T(8,128)(2,1)S(1)}, bf16[4,4,16,1536]{3,2,1,0:T(8,128)(2,1)}, u32[]{:S(2)}) copy-start(bf16[4,4,16,1536]{3,2,1,0:T(8,128)(2,1)} %param.19) | copy-start | bytes 2359300
  7.2 904.7 %all-reduce.5.cloned.1.call-start = ((), (), s32[]{:S(2)}) async-start(), calls=%async_computation | async-start | bytes 131072 | tf_op jit(solution)/shard_map/psum | solution.py:229
  7.2 14.3 %collective-permute-start = (bf16[4,4,16,1536]{3,2,1,0:T(8,128)(2,1)}, bf16[4,4,16,1536]{3,2,1,0:T(8,128)(2,1)S(1)}, u32[]{:S(2)}, u32[]{:S(2)}) collective-permute-start(bf16[4,4,16,1536]{3,2,1,0:T(8,128)(2,1)} %param.20), channel_id=1, source_target_pairs={{0,32},{32,64},{64,96},{96,128},{128,160},{160,192},{192,224},{1,3... | collective-permute-start | bytes 2359304 | tf_op jit(solution)/shard_map/ppermute | solution.py:15
  12.3 13.5 %collective-permute-start.1 = (bf16[4,4,16,1536]{3,2,1,0:T(8,128)(2,1)}, bf16[4,4,16,1536]{3,2,1,0:T(8,128)(2,1)S(1)}, u32[]{:S(2)}, u32[]{:S(2)}) collective-permute-start(bf16[4,4,16,1536]{3,2,1,0:T(8,128)(2,1)} %param.20), channel_id=1, source_target_pairs={{32,0},{64,32},{96,64},{128,96},{160,128},{192,160},{224,192},{33,... | collective-permute-start | bytes 2359304 | tf_op jit(solution)/shard_map/ppermute | solution.py:18
  26.8 113.1 %collective-permute-start.3 = (bf16[12,4,16,1536]{3,2,1,0:T(8,128)(2,1)}, bf16[12,4,16,1536]{3,2,1,0:T(8,128)(2,1)}, u32[]{:S(2)}, u32[]{:S(2)}) collective-permute-start(bf16[12,4,16,1536]{3,2,1,0:T(8,128)(2,1)} %constant_dynamic-update-slice_fusion), channel_id=1, source_target_pairs={{1,0},{2,1},{3,2},{4,3},{5,4},{6,5},{7,6},{8,7},{9,8},{10,9},{11,1... | collective-permute-start | bytes 7077896 | tf_op jit(solution)/shard_map/ppermute | solution.py:18
  28.1 111.8 %collective-permute-start.2 = (bf16[12,4,16,1536]{3,2,1,0:T(8,128)(2,1)}, bf16[12,4,16,1536]{3,2,1,0:T(8,128)(2,1)}, u32[]{:S(2)}, u32[]{:S(2)}) collective-permute-start(bf16[12,4,16,1536]{3,2,1,0:T(8,128)(2,1)} %constant_dynamic-update-slice_fusion), channel_id=1, source_target_pairs={{0,1},{1,2},{2,3},{3,4},{4,5},{5,6},{6,7},{7,8},{8,9},{9,10},{10,1... | collective-permute-start | bytes 7077896 | tf_op jit(solution)/shard_map/ppermute | solution.py:15
  42.8 106.8 %copy-start.9 = (s32[12,3]{0,1:T(4,128)S(1)}, s32[12,3]{0,1:T(4,128)}, u32[]{:S(2)}) copy-start(s32[12,3]{0,1:T(4,128)} %param.23) | copy-start | bytes 436
  149.6 4.3 copy-start.4
  167.3 4.4 copy-start.4
  183.8 1.2 copy-start.5
  185.1 4.5 copy-start.4
  202.9 4.3 copy-start.4
  220.6 4.3 copy-start.4
  238.3 4.3 copy-start.4
  256.1 4.5 copy-start.4
  272.7 1.2 copy-start.5
  273.9 4.3 copy-start.4
  291.6 4.3 copy-start.4
  309.3 4.4 copy-start.4
  325.9 1.3 copy-start.5
  327.1 4.4 copy-start.4
  344.9 4.4 copy-start.4
  372.4 51.6 %copy-start.8 = (bf16[3072,16]{0,1:T(8,128)(2,1)S(1)}, bf16[3072,16]{0,1:T(8,128)(2,1)}, u32[]{:S(2)}) copy-start(bf16[3072,16]{0,1:T(8,128)(2,1)} %param.28) | copy-start | bytes 294916
  378.7 82.8 %collective-permute-start.5 = (bf16[12,12,4,16,128]{4,3,2,1,0:T(8,128)(2,1)}, bf16[12,12,4,16,128]{4,3,2,1,0:T(8,128)(2,1)}, u32[]{:S(2)}, u32[]{:S(2)}) collective-permute-start(bf16[12,12,4,16,128]{4,3,2,1,0:T(8,128)(2,1)} %get-tuple-element.230), channel_id=1, source_target_pairs={{0,1},{1,2},{2,3},{3,4},{4,5},{5,6},{6,7},{7,8},{8,9},{9,10},{10,1... | collective-permute-start | bytes 7077896 | tf_op jit(solution)/shard_map/ppermute | solution.py:26
  421.4 148.9 %collective-permute-start.4 = (bf16[12,12,4,16,128]{4,3,2,1,0:T(8,128)(2,1)}, bf16[12,12,4,16,128]{4,3,2,1,0:T(8,128)(2,1)}, u32[]{:S(2)}, u32[]{:S(2)}) collective-permute-start(bf16[12,12,4,16,128]{4,3,2,1,0:T(8,128)(2,1)} %get-tuple-element.229), channel_id=1, source_target_pairs={{1,0},{2,1},{3,2},{4,3},{5,4},{6,5},{7,6},{8,7},{9,8},{10,9},{11,1... | collective-permute-start | bytes 7077896 | tf_op jit(solution)/shard_map/ppermute | solution.py:26
  577.7 65.5 %copy-start.3 = (f32[12,256,128]{1,2,0:T(8,128)S(1)}, f32[12,256,128]{1,2,0:T(8,128)}, u32[]{:S(2)}) copy-start(f32[12,256,128]{1,2,0:T(8,128)} %get-tuple-element.192) | copy-start | bytes 4718596
  577.7 66.9 %copy-start.10 = (bf16[16,1536]{1,0:T(8,128)(2,1)S(1)}, bf16[16,1536]{1,0:T(8,128)(2,1)}, u32[]{:S(2)}) copy-start(bf16[16,1536]{1,0:T(8,128)(2,1)} %param.29) | copy-start | bytes 147460
  579.3 71.6 %collective-permute-start.7 = (bf16[12,4,4,16,128]{4,3,2,1,0:T(8,128)(2,1)}, bf16[12,4,4,16,128]{4,3,2,1,0:T(8,128)(2,1)}, u32[]{:S(2)}, u32[]{:S(2)}) collective-permute-start(bf16[12,4,4,16,128]{4,3,2,1,0:T(8,128)(2,1)} %get-tuple-element.232), channel_id=1, source_target_pairs={{0,32},{32,64},{64,96},{96,128},{128,160},{160,192},{192,224},{1,3... | collective-permute-start | bytes 2359304 | tf_op jit(solution)/shard_map/ppermute | solution.py:26
  641.1 13.6 %collective-permute-start.6 = (bf16[12,4,4,16,128]{4,3,2,1,0:T(8,128)(2,1)}, bf16[12,4,4,16,128]{4,3,2,1,0:T(8,128)(2,1)}, u32[]{:S(2)}, u32[]{:S(2)}) collective-permute-start(bf16[12,4,4,16,128]{4,3,2,1,0:T(8,128)(2,1)} %get-tuple-element.231), channel_id=1, source_target_pairs={{32,0},{64,32},{96,64},{128,96},{160,128},{192,160},{224,192},{33,... | collective-permute-start | bytes 2359304 | tf_op jit(solution)/shard_map/ppermute | solution.py:26
  662.2 5.5 copy-start.7
  667.7 3.5 copy-start.2
  (10 other events, 11.9 us)
Sparse Core Ops, SparseCore 0:
  671.3 240.5 all-reduce.4
where the time goes:
time: 925 us; the launch traced here: 920 us
  waiting for transfers between devices  492 us (53%)
  starting transfers between devices  129 us (14%)
  matrix products  89.3 us (10%)
  other arithmetic  82 us (9%)
  local copies, waits for them, and re-layouts  81.4 us (9%)
  loops' own time  31 us (3%)
  between operations  15.5 us (2%)
    psum x1, waiting for transfers between devices, per_device(): grad_sketch = lax.psum(local_sketch, ('tm', 'height'))  240 us
    ppermute x4, waiting for transfers between devices, shifted(): return lax.ppermute(array, axis, pairs)  147 us
    ppermute x4, starting transfers between devices, shifted(): return lax.ppermute(array, axis, pairs)  108 us
    ppermute x2, waiting for transfers between devices, padded_2(): lax.ppermute(lax.slice_in_dim(block, 0, width, axis=dim), axis, backward)  98.3 us
    reshape x50, local copies, waits for them, and re-layouts, tile_rows(): shaped = block.reshape((frame_count, row_count, col_tiles, width) + rest)  38.7 us
    another operation x1, loops' own time, per_device(): text_part, head_out = lax.map(forward, head_ids)  31 us
    and x12, other arithmetic, window_mask(): inside & (row_tile + row_step >= 0) & (row_tile + row_step < row_tiles)  23 us
    dot_general x12, matrix products, forward(): jnp.einsum('cql,cqd->cld', image_probs, cot_head, preferred_element_type=...  22.2 us
  transfers between devices with their start and end apart: 9, of which 7 were waited for; matrix products, arithmetic and copies ran while one was open for 2% of the time, Pallas kernels for 0%

commit v1 on v0

--- a/solution.py
+++ b/solution.py
@@ -226,7 +226,7 @@
     local_sketch = count_sketch(
         (grad_down, grad_up, text_down_grad, text_up_grad), sketch_seed[0], SKETCH, sketch_scale
     )
-    grad_sketch = lax.psum(local_sketch, ("tm", "height"))
+    grad_sketch = jnp.sum(lax.all_gather(local_sketch, ("tm", "height")), axis=0)
     return (value_grad, grad_sketch)
 
 

time: 925 us -> 1450 us (1.57)
  waiting for transfers between devices: 492 us -> 986 us
  local copies, waits for them, and re-layouts: 81.4 us -> 98.1 us
    all_gather x0 -> x1, waiting for transfers between devices: none -> 733 us  [per_device(): lax.all_gather(local_sketch, ('tm', 'height'))]
    psum x1 -> x0, waiting for transfers between devices: 240 us -> none  [per_device(): grad_sketch = lax.psum(local_sketch, ('tm', 'height'))]
    all_gather x0 -> x1, local copies, waits for them, and re-layouts: none -> 18.2 us  [per_device(): lax.all_gather(local_sketch, ('tm', 'height'))]
  transfers between devices with their start and end apart: 9 -> 9, of which waited for: 7 -> 7; matrix products, arithmetic and copies ran while one was open for 2% -> 1% of each run, Pallas kernels for 0% -> 0%
where the time goes in v1:
time: 1450 us; the launch traced here: 1440 us
  waiting for transfers between devices  986 us (68%)
  starting transfers between devices  129 us (9%)
  local copies, waits for them, and re-layouts  98.1 us (7%)
  matrix products  89.3 us (6%)
  other arithmetic  89.2 us (6%)
  loops' own time  31 us (2%)
  between operations  15.5 us (1%)
    all_gather x1, waiting for transfers between devices, per_device(): lax.all_gather(local_sketch, ('tm', 'height'))  733 us
    ppermute x4, waiting for transfers between devices, shifted(): return lax.ppermute(array, axis, pairs)  147 us
    ppermute x4, starting transfers between devices, shifted(): return lax.ppermute(array, axis, pairs)  108 us
    ppermute x2, waiting for transfers between devices, padded_2(): lax.ppermute(lax.slice_in_dim(block, 0, width, axis=dim), axis, backward)  98.3 us
    reshape x50, local copies, waits for them, and re-layouts, tile_rows(): shaped = block.reshape((frame_count, row_count, col_tiles, width) + rest)  38.7 us
    another operation x1, loops' own time, per_device(): text_part, head_out = lax.map(forward, head_ids)  31 us
  transfers between devices with their start and end apart: 9, of which 7 were waited for; matrix products, arithmetic and copies ran while one was open for 1% of the time, Pallas kernels for 0%

profile of v1, /device:TPU:1, one launch (start us, length us, event | category | flops | bytes accessed | tf_op | source)
XLA Modules:
  0.0 1437.4 jit_solution(6029774690953000315)
XLA Ops:
  7.2 5.1 collective-permute-start
  12.3 1.9 collective-permute-start.1
  14.2 7.3 collective-permute-done
  22.5 2.1 constant_dynamic-update-slice_fusion.1
  28.1 12.5 collective-permute-start.2
  40.7 2.1 copy.66
  42.8 97.1 %collective-permute-done.3 = bf16[12,4,16,1536]{3,2,1,0:T(8,128)(2,1)} collective-permute-done((bf16[12,4,16,1536]{3,2,1,0:T(8,128)(2,1)}, bf16[12,4,16,1536]{3,2,1,0:T(8,128)(2,1)}, u32[]{:S(2)}, u32[]{:S(2)}) %collective-permute-start.3) | collective-permute-done | bytes 2359328 | tf_op jit(solution)/shard_map/ppermute | solution.py:18
  139.9 9.7 fusion.52
  149.6 213.1 %while.15 = (s32[]{:T(128)}, f32[12,256,128]{1,2,0:T(8,128)}, f32[12,12,12,16,128]{4,3,2,1,0:T(8,128)}, s32[12]{0:T(128)S(1)}, bf16[2,128,1536]{2,1,0:T(8,128)(2...) while((s32[]{:T(128)}, f32[12,256,128]{1,2,0:T(8,128)}, ...), condition=%wide.region_5.6_spmd, body=%wide.region_0.5_spmd.sunk | while | flops 499376128 | bytes 40042176 | solution.py:185
  169.7 1.9 dynamic-slice_bitcast_fusion.4
  187.6 2.0 dynamic-slice_bitcast_fusion.4
  193.3 1.9 compare_and_fusion.4
  228.6 1.9 compare_and_fusion.4
  258.5 2.0 dynamic-slice_bitcast_fusion.4
  347.4 2.0 dynamic-slice_bitcast_fusion.4
  362.7 9.7 convert.8
  372.4 6.3 fusion.75
  378.7 42.7 %collective-permute-start.5 = (bf16[12,12,4,16,128]{4,3,2,1,0:T(8,128)(2,1)}, bf16[12,12,4,16,128]{4,3,2,1,0:T(8,128)(2,1)}, u32[]{:S(2)}, u32[]{:S(2)}) collective-permute-start(bf16[12,12,4,16,128]{4,3,2,1,0:T(8,128)(2,1)} %get-tuple-element.230), channel_id=1, source_target_pairs={{0,1},{1,2},{2,3},{3,4},{4,5},{5,6},{6,7},{7,8},{8,9},{9,10},{10,1... | collective-permute-start | bytes 7077896 | tf_op jit(solution)/shard_map/ppermute | solution.py:26
  424.5 2.6 add_convert_fusion
  427.1 34.4 %collective-permute-done.5 = bf16[12,12,4,16,128]{4,3,2,1,0:T(8,128)(2,1)} collective-permute-done((bf16[12,12,4,16,128]{4,3,2,1,0:T(8,128)(2,1)}, bf16[12,12,4,16,128]{4,3,2,1,0:T(8,128)(2,1)}, u32[]{:S(2)}, u32[]{:S(2)}) %collective-permute-start.5) | collective-permute-done | bytes 2359328 | tf_op jit(solution)/shard_map/ppermute | solution.py:26
  461.5 108.8 %collective-permute-done.4 = bf16[12,12,4,16,128]{4,3,2,1,0:T(8,128)(2,1)} collective-permute-done((bf16[12,12,4,16,128]{4,3,2,1,0:T(8,128)(2,1)}, bf16[12,12,4,16,128]{4,3,2,1,0:T(8,128)(2,1)}, u32[]{:S(2)}, u32[]{:S(2)}) %collective-permute-start.4) | collective-permute-done | bytes 2359328 | tf_op jit(solution)/shard_map/ppermute | solution.py:26
  570.3 7.4 fusion.71
  579.3 61.7 %collective-permute-start.7 = (bf16[12,4,4,16,128]{4,3,2,1,0:T(8,128)(2,1)}, bf16[12,4,4,16,128]{4,3,2,1,0:T(8,128)(2,1)}, u32[]{:S(2)}, u32[]{:S(2)}) collective-permute-start(bf16[12,4,4,16,128]{4,3,2,1,0:T(8,128)(2,1)} %get-tuple-element.232), channel_id=1, source_target_pairs={{0,32},{32,64},{64,96},{96,128},{128,160},{160,192},{192,224},{1,3... | collective-permute-start | bytes 2359304 | tf_op jit(solution)/shard_map/ppermute | solution.py:26
  641.1 2.1 collective-permute-start.6
  644.6 2.0 fusion.77
  650.9 3.8 collective-permute-done.6
  654.7 2.2 fusion.54
  659.3 2.2 fusion.55
  662.2 3.7 fusion.56
  672.2 733.0 %all-gather.3.cloned.1.call-done = f32[4194304]{0:T(1024)} async-done(((f32[16384]{0:T(1024)}), f32[4194304]{0:T(1024)}) %all-gather.3.cloned.1.call-update) | async-done | bytes 16777232 | tf_op jit(solution)/shard_map/all_gather | solution.py:229
  1405.1 18.2 %reshape.281 = f32[256,16384]{1,0:T(8,128)} reshape(f32[4194304]{0:T(1024)} %all-gather.3.cloned.1.call-done) | data formatting | bytes 33554432 | tf_op jit(solution)/shard_map/all_gather | solution.py:229
  1423.3 7.2 reduce_sum.45
  (329 shorter events, 193.3 us)
Async XLA Ops:
  7.2 416.8 %copy-start = (bf16[256,3072]{1,0:T(8,128)(2,1)S(1)}, bf16[256,3072]{1,0:T(8,128)(2,1)}, u32[]{:S(2)}) copy-start(bf16[256,3072]{1,0:T(8,128)(2,1)} %param.18) | copy-start | bytes 4718596
  7.2 33.5 %copy-start.6 = (bf16[4,4,16,1536]{3,2,1,0:T(8,128)(2,1)S(1)}, bf16[4,4,16,1536]{3,2,1,0:T(8,128)(2,1)}, u32[]{:S(2)}) copy-start(bf16[4,4,16,1536]{3,2,1,0:T(8,128)(2,1)} %param.19) | copy-start | bytes 2359300
  7.2 1397.9 %all-gather.3.cloned.1.call-start = ((), (), s32[]{:S(2)}) async-start(), calls=%async_computation | async-start | bytes 16842752 | tf_op jit(solution)/shard_map/all_gather | solution.py:229
  7.2 14.3 collective-permute-start
  12.3 13.5 collective-permute-start.1
  26.8 113.1 %collective-permute-start.3 = (bf16[12,4,16,1536]{3,2,1,0:T(8,128)(2,1)}, bf16[12,4,16,1536]{3,2,1,0:T(8,128)(2,1)}, u32[]{:S(2)}, u32[]{:S(2)}) collective-permute-start(bf16[12,4,16,1536]{3,2,1,0:T(8,128)(2,1)} %constant_dynamic-update-slice_fusion), channel_id=1, source_target_pairs={{1,0},{2,1},{3,2},{4,3},{5,4},{6,5},{7,6},{8,7},{9,8},{10,9},{11,1... | collective-permute-start | bytes 7077896 | tf_op jit(solution)/shard_map/ppermute | solution.py:18
  28.1 111.8 %collective-permute-start.2 = (bf16[12,4,16,1536]{3,2,1,0:T(8,128)(2,1)}, bf16[12,4,16,1536]{3,2,1,0:T(8,128)(2,1)}, u32[]{:S(2)}, u32[]{:S(2)}) collective-permute-start(bf16[12,4,16,1536]{3,2,1,0:T(8,128)(2,1)} %constant_dynamic-update-slice_fusion), channel_id=1, source_target_pairs={{0,1},{1,2},{2,3},{3,4},{4,5},{5,6},{6,7},{7,8},{8,9},{9,10},{10,1... | collective-permute-start | bytes 7077896 | tf_op jit(solution)/shard_map/ppermute | solution.py:15
  42.8 106.8 %copy-start.9 = (s32[12,3]{0,1:T(4,128)S(1)}, s32[12,3]{0,1:T(4,128)}, u32[]{:S(2)}) copy-start(s32[12,3]{0,1:T(4,128)} %param.23) | copy-start | bytes 436
  149.6 4.3 copy-start.4
  167.3 4.4 copy-start.4
  183.8 1.2 copy-start.5
  185.1 4.5 copy-start.4
  202.9 4.3 copy-start.4
  220.6 4.3 copy-start.4
  238.3 4.3 copy-start.4
  256.1 4.5 copy-start.4
  272.7 1.2 copy-start.5
  273.9 4.3 copy-start.4
  291.6 4.3 copy-start.4
  309.3 4.4 copy-start.4
  325.9 1.3 copy-start.5
  327.1 4.4 copy-start.4
  344.9 4.4 copy-start.4
  372.4 51.6 %copy-start.8 = (bf16[3072,16]{0,1:T(8,128)(2,1)S(1)}, bf16[3072,16]{0,1:T(8,128)(2,1)}, u32[]{:S(2)}) copy-start(bf16[3072,16]{0,1:T(8,128)(2,1)} %param.28) | copy-start | bytes 294916
  378.7 82.8 %collective-permute-start.5 = (bf16[12,12,4,16,128]{4,3,2,1,0:T(8,128)(2,1)}, bf16[12,12,4,16,128]{4,3,2,1,0:T(8,128)(2,1)}, u32[]{:S(2)}, u32[]{:S(2)}) collective-permute-start(bf16[12,12,4,16,128]{4,3,2,1,0:T(8,128)(2,1)} %get-tuple-element.230), channel_id=1, source_target_pairs={{0,1},{1,2},{2,3},{3,4},{4,5},{5,6},{6,7},{7,8},{8,9},{9,10},{10,1... | collective-permute-start | bytes 7077896 | tf_op jit(solution)/shard_map/ppermute | solution.py:26
  421.4 148.9 %collective-permute-start.4 = (bf16[12,12,4,16,128]{4,3,2,1,0:T(8,128)(2,1)}, bf16[12,12,4,16,128]{4,3,2,1,0:T(8,128)(2,1)}, u32[]{:S(2)}, u32[]{:S(2)}) collective-permute-start(bf16[12,12,4,16,128]{4,3,2,1,0:T(8,128)(2,1)} %get-tuple-element.229), channel_id=1, source_target_pairs={{1,0},{2,1},{3,2},{4,3},{5,4},{6,5},{7,6},{8,7},{9,8},{10,9},{11,1... | collective-permute-start | bytes 7077896 | tf_op jit(solution)/shard_map/ppermute | solution.py:26
  577.7 65.5 %copy-start.3 = (f32[12,256,128]{1,2,0:T(8,128)S(1)}, f32[12,256,128]{1,2,0:T(8,128)}, u32[]{:S(2)}) copy-start(f32[12,256,128]{1,2,0:T(8,128)} %get-tuple-element.192) | copy-start | bytes 4718596
  577.7 66.9 %copy-start.10 = (bf16[16,1536]{1,0:T(8,128)(2,1)S(1)}, bf16[16,1536]{1,0:T(8,128)(2,1)}, u32[]{:S(2)}) copy-start(bf16[16,1536]{1,0:T(8,128)(2,1)} %param.29) | copy-start | bytes 147460
  579.3 71.6 %collective-permute-start.7 = (bf16[12,4,4,16,128]{4,3,2,1,0:T(8,128)(2,1)}, bf16[12,4,4,16,128]{4,3,2,1,0:T(8,128)(2,1)}, u32[]{:S(2)}, u32[]{:S(2)}) collective-permute-start(bf16[12,4,4,16,128]{4,3,2,1,0:T(8,128)(2,1)} %get-tuple-element.232), channel_id=1, source_target_pairs={{0,32},{32,64},{64,96},{96,128},{128,160},{160,192},{192,224},{1,3... | collective-permute-start | bytes 2359304 | tf_op jit(solution)/shard_map/ppermute | solution.py:26
  641.1 13.6 collective-permute-start.6
  662.2 5.5 copy-start.7
  667.7 3.5 copy-start.2
  (10 other events, 11.9 us)
Sparse Core Ops, SparseCore 0:
  671.3 733.7 all-gather.2
